TPU v7x, 32 devices: a whole 2x2x4 slice. The times are simulated.
32 devices in a mesh: dp: 4 (over x, core), sp: 8 (over z, y).
Axes of the slice: x: 2, y: 2, z: 4, core: 2. Of those that a mesh axis runs over, the one named last changes fastest.
Arguments:
- frames_in: bfloat16 [2048, 64, 256], P(('dp', 'sp')), may hold values from -6 to 6
- spatial_weight: bfloat16 [3, 3, 256, 256], replicated, may hold values from -0.125 to 0.125
- temporal_weight: bfloat16 [3, 256, 256], replicated, may hold values from -0.21875 to 0.21875
- cotangent: bfloat16 [2048, 64, 256], P(('dp', 'sp')), may hold values from -6 to 6
Outputs:
- block_out: bfloat16 [2048, 64, 256], P(('dp', 'sp'))
- grad_input: bfloat16 [2048, 64, 256], P(('dp', 'sp'))
- grad_spatial: float32 [3, 3, 256, 256], replicated
- grad_temporal: float32 [3, 256, 256], replicated
All inputs are finite; a program needn't handle non-finite values.
Results may differ from a plain program's by a relative error of at most 0.0049.
Values may be sent and summed in bfloat16 or wider, within the bound.
A program may use at most 128 MiB of HBM per device.

v0:
```python
import math
import jax
import jax.numpy as jnp
from jax import lax
from jax.sharding import PartitionSpec as P

H = 64
FRAMES = 4


def contract_rows(left, right):
    return lax.dot_general(
        left, right, (((0,), (0,)), ((), ())), preferred_element_type=jnp.float32
    )


def times_transpose(left, weight):
    return lax.dot_general(
        left, weight, (((1,), (1,)), ((), ())), preferred_element_type=jnp.float32
    )


def local(frames_in, spatial_weight, temporal_weight, cotangent):
    slab_rows, width_cells, channels = frames_in.shape
    sp_count = lax.axis_size("sp")

    def padded_rows(values):
        return jnp.pad(values, ((1, 1), (1, 1), (0, 0)))

    def flatten_rows(values):
        return values.reshape(-1, channels)

    padded_in = padded_rows(frames_in)
    pre = jnp.zeros((slab_rows * width_cells, channels), jnp.float32)
    for tap_row in range(3):
        for tap_col in range(3):
            window = flatten_rows(
                padded_in[tap_row : tap_row + slab_rows, tap_col : tap_col + width_cells]
            )
            pre = pre + jnp.dot(
                window, spatial_weight[tap_row, tap_col], preferred_element_type=jnp.float32
            )
    act = jax.nn.silu(pre).astype(jnp.bfloat16).reshape(slab_rows, width_cells, channels)

    def to_frames(values):
        return lax.all_to_all(values, "sp", split_axis=0, concat_axis=1, tiled=True)

    moved_act, moved_cot = (
        lax.all_to_all(act, "sp", split_axis=1, concat_axis=0, tiled=True),
        lax.all_to_all(cotangent, "sp", split_axis=1, concat_axis=0, tiled=True),
    )
    group_rows = slab_rows * sp_count
    stripe = width_cells // sp_count
    groups = group_rows // (FRAMES * H)
    act_clips = moved_act.reshape(groups, FRAMES, H * stripe, channels)
    cot_clips = moved_cot.reshape(groups, FRAMES, H * stripe, channels)
    act_padded = jnp.pad(act_clips, ((0, 0), (2, 0), (0, 0), (0, 0)))
    cot_padded = jnp.pad(cot_clips, ((0, 0), (0, 2), (0, 0), (0, 0)))
    temporal_sum = jnp.zeros(act_clips.shape, jnp.float32)
    act_grad_sum = jnp.zeros(act_clips.shape, jnp.float32)
    temporal_terms = []
    for tap_step in range(3):
        earlier = act_padded[:, 2 - tap_step : 2 - tap_step + FRAMES]
        temporal_sum = temporal_sum + jnp.einsum(
            "gfpc,cd->gfpd", earlier, temporal_weight[tap_step], preferred_element_type=jnp.float32
        )
        temporal_terms.append(
            jnp.einsum("gfpc,gfpd->cd", earlier, cot_clips, preferred_element_type=jnp.float32)
        )
        later = cot_padded[:, tap_step : tap_step + FRAMES]
        act_grad_sum = act_grad_sum + jnp.einsum(
            "gfpd,cd->gfpc", later, temporal_weight[tap_step], preferred_element_type=jnp.float32
        )
    temporal_out = to_frames(
        temporal_sum.astype(jnp.bfloat16).reshape(group_rows, stripe, channels)
    )
    grad_act = to_frames(act_grad_sum.astype(jnp.bfloat16).reshape(group_rows, stripe, channels))
    grad_temporal = jnp.stack(temporal_terms)
    grad_scale = 1.0 / math.sqrt(slab_rows * sp_count * lax.axis_size("dp") * width_cells)
    block_out = (frames_in.astype(jnp.float32) + temporal_out.astype(jnp.float32)).astype(
        jnp.bfloat16
    )
    sigma = jax.nn.sigmoid(pre)
    grad_pre = (
        flatten_rows(grad_act).astype(jnp.float32) * (sigma * (1.0 + pre * (1.0 - sigma)))
    ).astype(jnp.bfloat16)
    grad_padded = padded_rows(grad_pre.reshape(slab_rows, width_cells, channels))
    spatial_terms = []
    grad_in = flatten_rows(cotangent).astype(jnp.float32)
    for tap_row in range(3):
        for tap_col in range(3):
            window = flatten_rows(
                padded_in[tap_row : tap_row + slab_rows, tap_col : tap_col + width_cells]
            )
            spatial_terms.append(contract_rows(window, grad_pre))
            back_window = flatten_rows(
                grad_padded[
                    2 - tap_row : 2 - tap_row + slab_rows, 2 - tap_col : 2 - tap_col + width_cells
                ]
            )
            grad_in = grad_in + times_transpose(back_window, spatial_weight[tap_row, tap_col])
    grad_spatial = jnp.stack(spatial_terms).reshape(3, 3, channels, channels)
    grad_spatial, grad_temporal = lax.psum((grad_spatial, grad_temporal), ("dp", "sp"))
    grad_input = grad_in.astype(jnp.bfloat16).reshape(slab_rows, width_cells, channels)
    return (block_out, grad_input, grad_spatial * grad_scale, grad_temporal * grad_scale)


def solution(mesh):
    placed = (P(("dp", "sp"), None, None), P(), P(), P(("dp", "sp"), None, None))
    return jax.shard_map(
        local,
        mesh=mesh,
        in_specs=placed,
        out_specs=(P(("dp", "sp"), None, None), P(("dp", "sp"), None, None), P(), P()),
        check_vma=False,
    )
```

profile of v0, /device:TPU:0, one launch (start us, length us, event | category | flops | bytes accessed | tf_op | source)
XLA Modules:
  0.0 385.7 jit_solution(17746489602125472998)
XLA Ops:
  7.2 4.1 %copy.32 = bf16[64,64,256]{2,0,1:T(8,128)(2,1)} copy(bf16[64,64,256]{2,1,0:T(8,128)(2,1)} %param.7) | data formatting | bytes 4194304 | tf_op args[3]
  11.3 7.4 %all-to-all-start.2 = ((bf16[64,64,256]{2,0,1:T(8,128)(2,1)}), bf16[64,64,256]{2,0,1:T(8,128)(2,1)}, u32[]{:S(2)}, u32[]{:S(2)}) async-start(bf16[64,64,256]{2,0,1:T(8,128)(2,1)} %copy.32), calls=%async_computation.2 | async-start | bytes 4194304 | tf_op jit(solution)/shard_map/all_to_all | solution.py:50
  18.7 9.8 %pad_slice_fusion.10 = (bf16[64,64,256]{2,1,0:T(8,128)(2,1)}, bf16[64,64,256]{2,1,0:T(8,128)(2,1)}, bf16[64,64,256]{2,1,0:T(8,128)(2,1)}, bf16[64,64,256]{2,1,0:...) fusion(bf16[64,64,256]{2,1,0:T(8,128)(2,1)S(1)} %copy-done.3), kind=kLoop, calls=%fused_computation.46 | loop fusion | bytes 18874368 | tf_op jit(solution)/shard_map/slice | solution.py:38
  28.4 38.6 %all-to-all-done.2 = bf16[64,64,256]{2,0,1:T(8,128)(2,1)} async-done(((bf16[64,64,256]{2,0,1:T(8,128)(2,1)}), bf16[64,64,256]{2,0,1:T(8,128)(2,1)}, u32[]{:S(2)}, u32[]{:S(2)}) %all-to-all-start.2) | async-done | bytes 2097184 | tf_op jit(solution)/shard_map/all_to_all | solution.py:50
  67.0 2.9 copy.33
  69.9 0.7 fusion.38
  70.7 0.7 fusion.42
  71.4 2.1 add_convert_fusion
  73.5 4.8 %all-to-all-start.3 = ((bf16[512,8,256]{2,1,0:T(8,128)(2,1)}), bf16[512,8,256]{2,1,0:T(8,128)(2,1)}, u32[]{:S(2)}, u32[]{:S(2)}) async-start(bf16[512,8,256]{2,1,0:T(8,128)(2,1)} %bitcast.239), calls=%async_computation.3 | async-start | bytes 4194304 | tf_op jit(solution)/shard_map/all_to_all | solution.py:46
  78.3 2.4 fusion.63
  81.5 0.9 copy-done.16
  83.1 0.9 copy-done.13
  84.7 0.8 convolution_add_fusion.13
  85.5 0.8 copy-done.10
  87.0 0.9 copy-done.8
  88.6 0.9 copy-done.6
  89.4 2.7 convolution_add_fusion.10
  92.1 34.0 %all-to-all-done.3 = bf16[512,8,256]{2,1,0:T(8,128)(2,1)} async-done(((bf16[512,8,256]{2,1,0:T(8,128)(2,1)}), bf16[512,8,256]{2,1,0:T(8,128)(2,1)}, u32[]{:S(2)}, u32[]{:S(2)}) %all-to-all-start.3) | async-done | bytes 2097184 | tf_op jit(solution)/shard_map/all_to_all | solution.py:46
  126.1 2.0 convert_bitcast_fusion
  128.7 1.6 copy-done.23
  130.9 3.5 fusion.2
  134.4 2.5 copy.29
  137.0 4.9 %all-to-all-start = ((bf16[64,64,256]{2,0,1:T(8,128)(2,1)}), bf16[64,64,256]{2,0,1:T(8,128)(2,1)}, u32[]{:S(2)}, u32[]{:S(2)}) async-start(bf16[64,64,256]{2,0,1:T(8,128)(2,1)} %copy.29), calls=%async_computation | async-start | bytes 4194304 | tf_op jit(solution)/shard_map/all_to_all | solution.py:49
  141.9 3.1 fusion.35
  145.3 0.8 fusion.34
  146.1 0.8 copy-done.17
  146.9 0.8 fusion.33
  147.7 0.8 copy-done.14
  148.5 0.8 fusion.32
  149.3 1.0 fusion.31
  150.9 0.8 fusion.30
  151.7 0.8 copy-done.9
  152.5 0.8 fusion.29
  153.3 0.8 copy-done.7
  154.1 0.8 fusion.28
  154.9 0.8 copy-done.26
  155.7 0.8 fusion.27
  156.4 1.4 copy-done.24
  157.8 10.4 %pad_slice_fusion.2 = (bf16[64,64,256]{2,1,0:T(8,128)(2,1)}, bf16[64,64,256]{2,1,0:T(8,128)(2,1)S(1)}, bf16[64,64,256]{2,1,0:T(8,128)(2,1)S(1)}, bf16[64,64,256]...) fusion(bf16[64,64,256]{2,1,0:T(8,128)(2,1)S(1)} %bitcast.256), kind=kLoop, calls=%fused_computation.38 | loop fusion | bytes 18874368 | tf_op jit(solution)/shard_map/slice | solution.py:97
  168.3 0.8 convolution_add_fusion.8
  169.1 0.7 convolution_add_fusion.7
  169.8 0.7 convolution_add_fusion.6
  170.6 0.7 convolution_add_fusion.5
  171.3 2.8 convolution_add_fusion.4
  174.1 15.5 %all-to-all-done = bf16[64,64,256]{2,0,1:T(8,128)(2,1)} async-done(((bf16[64,64,256]{2,0,1:T(8,128)(2,1)}), bf16[64,64,256]{2,0,1:T(8,128)(2,1)}, u32[]{:S(2)}, u32[]{:S(2)}) %all-to-all-start) | async-done | bytes 2097184 | tf_op jit(solution)/shard_map/all_to_all | solution.py:49
  189.6 3.0 copy.30
  192.7 0.8 fusion.12
  194.4 0.7 fusion.44
  195.1 2.0 add_convert_fusion.1
  197.1 4.4 %all-to-all-start.1 = ((bf16[512,8,256]{2,1,0:T(8,128)(2,1)}), bf16[512,8,256]{2,1,0:T(8,128)(2,1)}, u32[]{:S(2)}, u32[]{:S(2)}) async-start(bf16[512,8,256]{2,1,0:T(8,128)(2,1)} %bitcast.238), calls=%async_computation.1 | async-start | bytes 4194304 | tf_op jit(solution)/shard_map/all_to_all | solution.py:46
  202.0 1.3 copy-done.2
  203.3 0.7 fusion.17
  204.1 0.7 fusion.22
  204.8 0.9 pad_maximum_fusion
  205.8 3.7 convolution_add_fusion.3
  209.5 0.8 convolution_add_fusion.2
  210.3 0.8 copy-done.15
  211.1 0.7 convolution_add_fusion.1
  211.8 0.8 copy-done.12
  212.7 2.1 fusion
  214.8 154.8 %all-reduce.7.cloned.1.call-done = (f32[3,3,256,256]{3,2,1,0:T(8,128)}, f32[3,256,256]{2,1,0:T(8,128)}) async-done(((f32[3,3,256,256]{3,2,1,0:T(8,128)}, f32[3,256,256]{2,1,0:T(8,128)}), (f32[3,3,256,256]{3,2,1,0:T(8,128)}, f32[3,256,256]{2,1,0:T(8,128)})) %all-reduce.7.cloned.1.call-update) | async-done | bytes 3145744 | tf_op jit(solution)/shard_map/psum | solution.py:103
  369.6 2.1 broadcast_multiply_fusion.1
  371.6 3.4 broadcast_multiply_fusion
  375.1 3.6 fusion.1
  (54 shorter events, 7.3 us)
Async XLA Ops:
  11.2 7.4 %copy-start.3 = (bf16[64,64,256]{2,1,0:T(8,128)(2,1)S(1)}, bf16[64,64,256]{2,1,0:T(8,128)(2,1)}, u32[]{:S(2)}) copy-start(bf16[64,64,256]{2,1,0:T(8,128)(2,1)} %param.4) | copy-start | bytes 6291460
  11.3 55.8 %all-to-all-start.2 = ((bf16[64,64,256]{2,0,1:T(8,128)(2,1)}), bf16[64,64,256]{2,0,1:T(8,128)(2,1)}, u32[]{:S(2)}, u32[]{:S(2)}) async-start(bf16[64,64,256]{2,0,1:T(8,128)(2,1)} %copy.32), calls=%async_computation.2 | async-start | bytes 4194304 | tf_op jit(solution)/shard_map/all_to_all | solution.py:50
  67.0 2.9 copy-start.27
  69.9 1.5 copy-start
  73.5 4.8 %copy-start.22 = (bf16[3,3,256,256]{3,2,1,0:T(8,128)(2,1)S(1)}, bf16[3,3,256,256]{3,2,1,0:T(8,128)(2,1)}, u32[]{:S(2)}) copy-start(bf16[3,3,256,256]{3,2,1,0:T(8,128)(2,1)} %param.5) | copy-start | bytes 3538948
  73.5 52.6 %all-to-all-start.3 = ((bf16[512,8,256]{2,1,0:T(8,128)(2,1)}), bf16[512,8,256]{2,1,0:T(8,128)(2,1)}, u32[]{:S(2)}, u32[]{:S(2)}) async-start(bf16[512,8,256]{2,1,0:T(8,128)(2,1)} %bitcast.239), calls=%async_computation.3 | async-start | bytes 4194304 | tf_op jit(solution)/shard_map/all_to_all | solution.py:46
  78.3 2.5 copy-start.19
  80.8 1.6 copy-start.16
  82.4 1.6 copy-start.13
  84.7 1.6 copy-start.10
  86.3 1.6 copy-start.8
  87.8 1.6 copy-start.6
  128.1 2.2 copy-start.23
  128.1 2.9 copy-start.25
  137.0 52.7 %all-to-all-start = ((bf16[64,64,256]{2,0,1:T(8,128)(2,1)}), bf16[64,64,256]{2,0,1:T(8,128)(2,1)}, u32[]{:S(2)}, u32[]{:S(2)}) async-start(bf16[64,64,256]{2,0,1:T(8,128)(2,1)} %copy.29), calls=%async_computation | async-start | bytes 4194304 | tf_op jit(solution)/shard_map/all_to_all | solution.py:49
  141.9 3.1 copy-start.20
  141.9 3.5 copy-start.21
  145.3 1.6 copy-start.17
  146.9 1.6 copy-start.14
  149.3 1.6 copy-start.11
  150.9 1.6 copy-start.9
  152.5 1.6 copy-start.7
  154.1 1.6 copy-start.26
  156.4 1.4 copy-start.24
  157.8 10.5 %copy-start.5 = (bf16[64,64,256]{2,1,0:T(8,128)(2,1)S(1)}, bf16[64,64,256]{2,1,0:T(8,128)(2,1)}, u32[]{:S(2)}) copy-start(bf16[64,64,256]{2,1,0:T(8,128)(2,1)} %param.7) | copy-start | bytes 6291460
  189.6 3.0 copy-start.1
  192.7 1.0 copy-start.28
  197.1 178.0 %all-to-all-start.1 = ((bf16[512,8,256]{2,1,0:T(8,128)(2,1)}), bf16[512,8,256]{2,1,0:T(8,128)(2,1)}, u32[]{:S(2)}, u32[]{:S(2)}) async-start(bf16[512,8,256]{2,1,0:T(8,128)(2,1)} %bitcast.238), calls=%async_computation.1 | async-start | bytes 4194304 | tf_op jit(solution)/shard_map/all_to_all | solution.py:46
  201.5 168.1 %all-reduce.7.cloned.1.call-start = ((), (), s32[]{:S(2)}) async-start(), calls=%async_computation.4 | async-start | bytes 6291456 | tf_op jit(solution)/shard_map/psum | solution.py:103
  201.7 1.6 copy-start.2
  205.8 3.7 copy-start.18
  209.5 1.6 copy-start.15
  211.1 1.6 copy-start.12
  371.6 3.4 copy-start.4
Sparse Core Ops, SparseCore 0:
  208.5 160.9 all-reduce.6
where the time goes:
time: 393 us; the launch traced here: 386 us
  waiting for transfers between devices  243 us (62%)
  local copies, waits for them, and re-layouts  49.7 us (13%)
  matrix products  44.8 us (11%)
  starting transfers between devices  21.7 us (6%)
  between operations  14.7 us (4%)
  other arithmetic  12 us (3%)
    psum x1, waiting for transfers between devices, local(): lax.psum((grad_spatial, grad_temporal), ('dp', 'sp'))  155 us
    all_to_all x1, waiting for transfers between devices, local(): lax.all_to_all(cotangent, 'sp', split_axis=1, concat_axis=0, tiled=True)  38.6 us
    all_to_all x2, waiting for transfers between devices, to_frames(): return lax.all_to_all(values, 'sp', split_axis=0, concat_axis=1, tiled=True)  34 us
    unnamed x59, local copies, waits for them, and re-layouts  20.2 us
    all_to_all x1, waiting for transfers between devices, local(): lax.all_to_all(act, 'sp', split_axis=1, concat_axis=0, tiled=True)  15.5 us
    dot_general x9, matrix products, times_transpose(): lax.dot_general(left, weight, (((1,), (1,)), ((), ())), preferred_element...  13.1 us
    dot_general x9, matrix products, local(): jnp.dot(window, spatial_weight[tap_row, tap_col], preferred_element_type=...  13 us
    slice x1, local copies, waits for them, and re-layouts, local(): grad_padded[2 - tap_row:2 - tap_row + slab_rows, 2 - tap_col:2 - tap_col...  10.4 us
  transfers between devices with their start and end apart: 5, of which 4 were waited for; matrix products, arithmetic and copies ran while one was open for 16% of the time, Pallas kernels for 0%

commit v1 on v0

--- a/solution.py
+++ b/solution.py
@@ -100,7 +100,7 @@
             )
             grad_in = grad_in + times_transpose(back_window, spatial_weight[tap_row, tap_col])
     grad_spatial = jnp.stack(spatial_terms).reshape(3, 3, channels, channels)
-    grad_spatial, grad_temporal = lax.psum((grad_spatial, grad_temporal), ("dp", "sp"))
+    grad_spatial, grad_temporal = lax.psum(lax.psum((grad_spatial, grad_temporal), "sp"), "dp")
     grad_input = grad_in.astype(jnp.bfloat16).reshape(slab_rows, width_cells, channels)
     return (block_out, grad_input, grad_spatial * grad_scale, grad_temporal * grad_scale)
 

time: 393 us -> 453 us (1.15)
  waiting for transfers between devices: 243 us -> 297 us
  matrix products: 44.8 us -> 52.9 us
    psum x1 -> x2, waiting for transfers between devices: 155 us -> 205 us  [the longest x1 145 us: local(): lax.psum((grad_spatial, grad_temporal), 'sp')]
    dot_general x3, matrix products: 3.44 us -> 8.3 us  [local(): jnp.einsum('gfpc,cd->gfpd', earlier, temporal_weight[tap_step], preferred...]
    unnamed x59 -> x69, local copies, waits for them, and re-layouts: 20.2 us -> 19.6 us
  transfers between devices with their start and end apart: 5 -> 6, of which waited for: 4 -> 5; matrix products, arithmetic and copies ran while one was open for 16% -> 14% of each run, Pallas kernels for 0% -> 0%
where the time goes in v1:
time: 453 us; the launch traced here: 446 us
  waiting for transfers between devices  297 us (66%)
  matrix products  52.9 us (12%)
  local copies, waits for them, and re-layouts  48.7 us (11%)
  starting transfers between devices  21.9 us (5%)
  between operations  14.7 us (3%)
  other arithmetic  10.8 us (2%)
    psum x1, waiting for transfers between devices, local(): lax.psum((grad_spatial, grad_temporal), 'sp')  145 us
    psum x1, waiting for transfers between devices, local(): lax.psum(lax.psum((grad_spatial, grad_temporal), 'sp'), 'dp')  59.8 us
    all_to_all x1, waiting for transfers between devices, local(): lax.all_to_all(cotangent, 'sp', split_axis=1, concat_axis=0, tiled=True)  38.6 us
    all_to_all x2, waiting for transfers between devices, to_frames(): return lax.all_to_all(values, 'sp', split_axis=0, concat_axis=1, tiled=True)  34 us
    all_to_all x1, waiting for transfers between devices, local(): lax.all_to_all(act, 'sp', split_axis=1, concat_axis=0, tiled=True)  19.9 us
    unnamed x69, local copies, waits for them, and re-layouts  19.6 us
    dot_general x9, matrix products, times_transpose(): lax.dot_general(left, weight, (((1,), (1,)), ((), ())), preferred_element...  16.6 us
    dot_general x9, matrix products, local(): jnp.dot(window, spatial_weight[tap_row, tap_col], preferred_element_type=...  12.9 us
  transfers between devices with their start and end apart: 6, of which 5 were waited for; matrix products, arithmetic and copies ran while one was open for 14% of the time, Pallas kernels for 0%

profile of v1, /device:TPU:0, one launch (start us, length us, event | category | flops | bytes accessed | tf_op | source)
XLA Modules:
  0.0 446.2 jit_solution(15040755272637693357)
XLA Ops:
  7.2 4.1 copy.32
  11.3 7.4 %all-to-all-start.2 = ((bf16[64,64,256]{2,0,1:T(8,128)(2,1)}), bf16[64,64,256]{2,0,1:T(8,128)(2,1)}, u32[]{:S(2)}, u32[]{:S(2)}) async-start(bf16[64,64,256]{2,0,1:T(8,128)(2,1)} %copy.32), calls=%async_computation.2 | async-start | bytes 4194304 | tf_op jit(solution)/shard_map/all_to_all | solution.py:50
  18.7 9.8 %pad_slice_fusion.10 = (bf16[64,64,256]{2,1,0:T(8,128)(2,1)}, bf16[64,64,256]{2,1,0:T(8,128)(2,1)}, bf16[64,64,256]{2,1,0:T(8,128)(2,1)}, bf16[64,64,256]{2,1,0:...) fusion(bf16[64,64,256]{2,1,0:T(8,128)(2,1)S(1)} %copy-done.2), kind=kLoop, calls=%fused_computation.46 | loop fusion | bytes 18874368 | tf_op jit(solution)/shard_map/slice | solution.py:38
  28.5 38.6 %all-to-all-done.2 = bf16[64,64,256]{2,0,1:T(8,128)(2,1)} async-done(((bf16[64,64,256]{2,0,1:T(8,128)(2,1)}), bf16[64,64,256]{2,0,1:T(8,128)(2,1)}, u32[]{:S(2)}, u32[]{:S(2)}) %all-to-all-start.2) | async-done | bytes 2097184 | tf_op jit(solution)/shard_map/all_to_all | solution.py:50
  67.0 2.9 copy.33
  69.9 0.7 fusion.38
  71.4 2.1 add_convert_fusion
  73.5 4.8 %all-to-all-start.3 = ((bf16[512,8,256]{2,1,0:T(8,128)(2,1)}), bf16[512,8,256]{2,1,0:T(8,128)(2,1)}, u32[]{:S(2)}, u32[]{:S(2)}) async-start(bf16[512,8,256]{2,1,0:T(8,128)(2,1)} %bitcast.239), calls=%async_computation.3 | async-start | bytes 4194304 | tf_op jit(solution)/shard_map/all_to_all | solution.py:46
  78.3 2.4 fusion.63
  81.5 0.9 copy-done.19
  83.1 0.9 copy-done.17
  84.7 0.8 convolution_add_fusion.13
  85.5 0.8 copy-done.15
  87.0 0.9 copy-done.13
  88.6 0.9 copy-done.11
  89.4 2.7 convolution_add_fusion.10
  92.1 34.0 %all-to-all-done.3 = bf16[512,8,256]{2,1,0:T(8,128)(2,1)} async-done(((bf16[512,8,256]{2,1,0:T(8,128)(2,1)}), bf16[512,8,256]{2,1,0:T(8,128)(2,1)}, u32[]{:S(2)}, u32[]{:S(2)}) %all-to-all-start.3) | async-done | bytes 2097184 | tf_op jit(solution)/shard_map/all_to_all | solution.py:46
  126.1 2.0 convert_bitcast_fusion
  128.7 1.6 copy-done.28
  130.9 3.5 fusion.2
  134.4 2.5 copy.29
  136.9 4.4 all-to-all-start
  141.9 3.1 fusion.35
  145.4 0.8 fusion.34
  146.1 0.8 copy-done.20
  147.0 0.8 fusion.33
  147.7 0.8 copy-done.18
  148.5 0.8 fusion.32
  149.3 1.0 fusion.31
  150.9 0.8 fusion.30
  151.7 0.8 copy-done.14
  152.5 0.8 fusion.29
  153.3 0.8 copy-done.12
  154.1 0.8 fusion.28
  154.9 0.8 copy-done.31
  155.7 0.8 fusion.27
  156.5 10.0 %pad_slice_fusion.2 = (bf16[64,64,256]{2,1,0:T(8,128)(2,1)}, bf16[64,64,256]{2,1,0:T(8,128)(2,1)}, bf16[64,64,256]{2,1,0:T(8,128)(2,1)}, bf16[64,64,256]{2,1,0:T...) fusion(bf16[64,64,256]{2,1,0:T(8,128)(2,1)S(1)} %bitcast.240), kind=kLoop, calls=%fused_computation.38 | loop fusion | bytes 18874368 | tf_op jit(solution)/shard_map/slice | solution.py:97
  166.4 2.7 convolution_add_fusion.8
  169.1 19.9 %all-to-all-done = bf16[64,64,256]{2,0,1:T(8,128)(2,1)} async-done(((bf16[64,64,256]{2,0,1:T(8,128)(2,1)}), bf16[64,64,256]{2,0,1:T(8,128)(2,1)}, u32[]{:S(2)}, u32[]{:S(2)}) %all-to-all-start) | async-done | bytes 2097184 | tf_op jit(solution)/shard_map/all_to_all | solution.py:49
  189.1 3.0 copy.30
  192.1 0.8 fusion.12
  192.9 3.6 fusion.40
  196.8 0.7 fusion.17
  197.5 0.7 fusion.22
  198.3 0.9 pad_maximum_fusion
  199.3 1.8 fusion.44
  201.5 2.9 add_convert_fusion.1
  204.4 4.5 %all-to-all-start.1 = ((bf16[512,8,256]{2,1,0:T(8,128)(2,1)}), bf16[512,8,256]{2,1,0:T(8,128)(2,1)}, u32[]{:S(2)}, u32[]{:S(2)}) async-start(bf16[512,8,256]{2,1,0:T(8,128)(2,1)} %bitcast.238), calls=%async_computation.1 | async-start | bytes 4194304 | tf_op jit(solution)/shard_map/all_to_all | solution.py:46
  209.2 3.1 convolution_add_fusion.7
  212.3 0.7 convolution_add_fusion.6
  213.0 0.8 copy-done.24
  213.9 0.7 convolution_add_fusion.5
  214.6 0.9 copy-done.7
  215.5 0.7 convolution_add_fusion.4
  216.3 0.8 copy-done.23
  217.1 2.7 convolution_add_fusion.3
  219.8 144.9 %all-reduce.9.cloned.1.call-done = (f32[3,3,256,256]{3,2,1,0:T(8,128)}, f32[3,256,256]{2,1,0:T(8,128)}) async-done(((f32[3,3,256,256]{3,2,1,0:T(8,128)}, f32[3,256,256]{2,1,0:T(8,128)}), (f32[3,3,256,256]{3,2,1,0:T(8,128)}, f32[3,256,256]{2,1,0:T(8,128)})) %all-reduce.9.cloned.1.call-update) | async-done | bytes 3145744 | tf_op jit(solution)/shard_map/psum | solution.py:103
  364.7 3.1 convolution_add_fusion.2
  368.5 0.8 copy-done.8
  369.4 2.1 fusion
  371.4 3.6 fusion.1
  375.1 59.8 %all-reduce.11.cloned.1.call-done = (f32[3,3,256,256]{3,2,1,0:T(8,128)}, f32[3,256,256]{2,1,0:T(8,128)}) async-done(((f32[3,3,256,256]{3,2,1,0:T(8,128)}, f32[3,256,256]{2,1,0:T(8,128)}), (f32[3,3,256,256]{3,2,1,0:T(8,128)}, f32[3,256,256]{2,1,0:T(8,128)})) %all-reduce.11.cloned.1.call-update) | async-done | bytes 3145744 | tf_op jit(solution)/shard_map/psum | solution.py:103
  434.8 3.3 broadcast_multiply_fusion
  438.2 0.9 broadcast_multiply_fusion.1
  (67 shorter events, 8.9 us)
Async XLA Ops:
  11.2 7.4 %copy-start.2 = (bf16[64,64,256]{2,1,0:T(8,128)(2,1)S(1)}, bf16[64,64,256]{2,1,0:T(8,128)(2,1)}, u32[]{:S(2)}) copy-start(bf16[64,64,256]{2,1,0:T(8,128)(2,1)} %param.4) | copy-start | bytes 6291460
  11.3 55.8 %all-to-all-start.2 = ((bf16[64,64,256]{2,0,1:T(8,128)(2,1)}), bf16[64,64,256]{2,0,1:T(8,128)(2,1)}, u32[]{:S(2)}, u32[]{:S(2)}) async-start(bf16[64,64,256]{2,0,1:T(8,128)(2,1)} %copy.32), calls=%async_computation.2 | async-start | bytes 4194304 | tf_op jit(solution)/shard_map/all_to_all | solution.py:50
  67.0 2.9 copy-start.32
  69.9 1.5 copy-start
  73.5 4.8 %copy-start.27 = (bf16[3,3,256,256]{3,2,1,0:T(8,128)(2,1)S(1)}, bf16[3,3,256,256]{3,2,1,0:T(8,128)(2,1)}, u32[]{:S(2)}) copy-start(bf16[3,3,256,256]{3,2,1,0:T(8,128)(2,1)} %param.5) | copy-start | bytes 3538948
  73.5 52.6 %all-to-all-start.3 = ((bf16[512,8,256]{2,1,0:T(8,128)(2,1)}), bf16[512,8,256]{2,1,0:T(8,128)(2,1)}, u32[]{:S(2)}, u32[]{:S(2)}) async-start(bf16[512,8,256]{2,1,0:T(8,128)(2,1)} %bitcast.239), calls=%async_computation.3 | async-start | bytes 4194304 | tf_op jit(solution)/shard_map/all_to_all | solution.py:46
  78.3 2.5 copy-start.21
  80.8 1.6 copy-start.19
  82.4 1.6 copy-start.17
  84.7 1.6 copy-start.15
  86.3 1.6 copy-start.13
  87.8 1.6 copy-start.11
  128.1 2.2 copy-start.28
  128.1 2.9 copy-start.30
  136.9 52.2 %all-to-all-start = ((bf16[64,64,256]{2,0,1:T(8,128)(2,1)}), bf16[64,64,256]{2,0,1:T(8,128)(2,1)}, u32[]{:S(2)}, u32[]{:S(2)}) async-start(bf16[64,64,256]{2,0,1:T(8,128)(2,1)} %copy.29), calls=%async_computation | async-start | bytes 4194304 | tf_op jit(solution)/shard_map/all_to_all | solution.py:49
  141.3 223.3 %all-reduce.9.cloned.1.call-start = ((), (), s32[]{:S(2)}) async-start(), calls=%async_computation.4 | async-start | bytes 6291456 | tf_op jit(solution)/shard_map/psum | solution.py:103
  141.9 3.1 copy-start.6
  141.9 3.5 copy-start.22
  145.4 1.6 copy-start.20
  147.0 1.6 copy-start.18
  149.3 1.6 copy-start.16
  150.9 1.6 copy-start.14
  152.5 1.6 copy-start.12
  154.1 1.6 copy-start.31
  156.4 10.0 %copy-start.29 = (f32[9,256,256]{2,1,0:T(8,128)}, f32[9,256,256]{2,1,0:T(8,128)S(1)}, u32[]{:S(2)}) copy-start(f32[9,256,256]{2,1,0:T(8,128)S(1)} %fusion.27) | copy-start | bytes 7077892
  156.4 10.0 %copy-start.5 = (bf16[64,64,256]{2,1,0:T(8,128)(2,1)S(1)}, bf16[64,64,256]{2,1,0:T(8,128)(2,1)}, u32[]{:S(2)}) copy-start(bf16[64,64,256]{2,1,0:T(8,128)(2,1)} %param.7) | copy-start | bytes 6291460
  189.1 3.0 copy-start.1
  199.2 2.3 copy-start.4
  204.4 4.7 %copy-start.26 = (bf16[64,64,256]{2,1,0:T(8,128)(2,1)S(1)}, bf16[64,64,256]{2,1,0:T(8,128)(2,1)}, u32[]{:S(2)}) copy-start(bf16[64,64,256]{2,1,0:T(8,128)(2,1)} %get-tuple-element.13) | copy-start | bytes 6291460
  204.4 167.0 %all-to-all-start.1 = ((bf16[512,8,256]{2,1,0:T(8,128)(2,1)}), bf16[512,8,256]{2,1,0:T(8,128)(2,1)}, u32[]{:S(2)}, u32[]{:S(2)}) async-start(bf16[512,8,256]{2,1,0:T(8,128)(2,1)} %bitcast.238), calls=%async_computation.1 | async-start | bytes 4194304 | tf_op jit(solution)/shard_map/all_to_all | solution.py:46
  208.9 225.9 %all-reduce.11.cloned.1.call-start = ((), (), s32[]{:S(2)}) async-start(), calls=%async_computation.5 | async-start | bytes 6291456 | tf_op jit(solution)/shard_map/psum | solution.py:103
  209.2 3.1 copy-start.25
  212.3 1.6 copy-start.24
  213.9 1.6 copy-start.7
  215.5 1.6 copy-start.23
  219.8 144.9 %copy-start.10 = (bf16[64,64,256]{2,1,0:T(8,128)(2,1)S(1)}, bf16[64,64,256]{2,1,0:T(8,128)(2,1)}, u32[]{:S(2)}) copy-start(bf16[64,64,256]{2,1,0:T(8,128)(2,1)} %get-tuple-element.17) | copy-start | bytes 6291460
  364.7 3.1 copy-start.9
  367.8 1.6 copy-start.8
  369.4 2.1 copy-start.3
  434.8 3.4 copy-start.33
Sparse Core Ops, SparseCore 0:
  199.4 165.2 all-reduce.8
  367.3 67.4 all-reduce.10
